TPU v7x, 32 devices: a whole 2x2x4 slice. The times are simulated.
32 devices in a mesh: dp: 8 (over z, y), group: 4 (over x, core).
Axes of the slice: x: 2, y: 2, z: 4, core: 2. Of those that a mesh axis runs over, the one named last changes fastest.
Arguments:
- params: float32 [1774080], P('group')
- moment1: float32 [1774080], P('group'), may hold values from -0.3 to 0.3
- moment2: float32 [1774080], P('group'), may hold values from 0.0001 to 0.01
- image_in: bfloat16 [64, 197, 384], P(('dp', 'group'))
- cotangent: bfloat16 [64, 197, 384], P(('dp', 'group')), may hold values from -6 to 6
- image_counts: int32 [32], P(('dp', 'group')), may hold values from 1 to 2, as said below
Outputs:
- block_out: bfloat16 [64, 197, 384], P(('dp', 'group'))
- input_grad: bfloat16 [64, 197, 384], P(('dp', 'group'))
- param_grad: float32 [1774080], P('group')
- new_params: float32 [1774080], P('group')
- new_moment1: float32 [1774080], P('group')
- new_moment2: float32 [1774080], P('group')
Inputs may be any that keep to these rules, and one draw needn't show every extreme that they name: image_counts gives each device the number of its slots, taken from the first, that hold live images; some device has 2 and some device has 1.
All inputs are finite; a program needn't handle non-finite values.
Results may differ from a plain program's by a relative error of at most 0.0095.
The roundings to bfloat16 on the way count: a program that leaves them out, or rounds other values in their place, can miss the bound.
Values sent between devices are 32-bit elements; how exact they have to be, the bound alone decides.
A program may use at most 128 MiB of HBM per device.

v0:
```python
import functools
import math

import jax
import jax.numpy as jnp
from jax import lax
from jax.experimental import pallas as pl
from jax.experimental.pallas import tpu as pltpu
from jax.sharding import PartitionSpec as P

D = 384
HEADS = 6
HEAD_DIM = 64
FF = 1536
STEP = 5
LANES = 128
MESH = pl.DeviceIdType.MESH
LOW = jnp.bfloat16
F32 = jnp.float32

SEGMENTS = [
    ("gain_a", 1, D),
    ("shift_a", 1, D),
    ("input", D, 3 * D),
    ("query_bias", 1, D),
    ("value_bias", 1, D),
    ("output", D, D),
    ("output_bias", 1, D),
    ("gain_b", 1, D),
    ("shift_b", 1, D),
    ("up", D, FF),
    ("up_bias", 1, FF),
    ("down", FF, D),
    ("down_bias", 1, D),
]


def starts_of():
    row, table = 0, {}
    for name, rows, columns in SEGMENTS:
        table[name] = row
        row += rows * columns // LANES
    return table


STARTS = starts_of()


class Layout:
    def __init__(self, shard, group, dp):
        self.real = shard // LANES
        self.group = group
        self.dp = dp
        unit = 8 * dp
        units = -(-self.real // unit)
        self.chunks = max(n for n in range(1, 12) if units % n == 0)
        self.padded = units * unit
        self.chunk = self.padded // self.chunks

    def pieces(self, start, stride, count):
        i, found = 0, []
        while i < count:
            row = start + stride * i
            shard = row // self.real
            n = min(count - i, ((shard + 1) * self.real - 1 - row) // stride + 1)
            found.append((shard * self.padded + row - shard * self.real, i, n))
            i += n
        return found


def gather_kernel(lay, own_ref, full_ref, sx, rx, sy, ry, sc, rc, so, ro, local_sem):
    d, g = lax.axis_index("dp"), lax.axis_index("group")
    half = d % 2
    core = {"dp": d, "group": g + 1 - 2 * (g % 2)}
    far_g = g + 2 - 4 * ((g // 2) % 2)
    far = {"dp": d, "group": far_g}
    side = {"dp": d + 1 - 2 * half, "group": g}
    barrier = pltpu.get_barrier_semaphore()
    for other in (core, far, side):
        pl.semaphore_signal(barrier, inc=1, device_id=other, device_id_type=MESH)
    pl.semaphore_wait(barrier, 3)

    piece = lay.chunk // 2
    half_rows = lay.padded // 2

    def rows(which, c):
        return pl.ds(pl.multiple_of(which * half_rows + c * piece, 8), piece)

    def send(src, shard, rows_at, s, r, other):
        copy = pltpu.make_async_remote_copy(
            src_ref=src,
            dst_ref=full_ref.at[shard, rows_at],
            send_sem=s,
            recv_sem=r,
            device_id=other,
            device_id_type=MESH,
        )
        copy.start()
        return copy

    def arrival(shard, rows_at, s, r, other):
        return pltpu.make_async_remote_copy(
            src_ref=full_ref.at[shard, rows_at],
            dst_ref=full_ref.at[shard, rows_at],
            send_sem=s,
            recv_sem=r,
            device_id=other,
            device_id_type=MESH,
        )

    sends = []
    xs = []
    for c in range(lay.chunks):
        at = rows(half, c)
        xs.append(send(own_ref.at[at], g, at, sx.at[c], rx.at[c], far))
    mine = pltpu.make_async_copy(own_ref, full_ref.at[g], local_sem)
    mine.start()
    own = pltpu.make_async_remote_copy(
        src_ref=own_ref,
        dst_ref=full_ref.at[g],
        send_sem=so,
        recv_sem=ro,
        device_id=core,
        device_id_type=MESH,
    )
    own.start()
    ys, cs = [], []
    for c in range(lay.chunks):
        at = rows(half, c)
        arrival(far_g, at, sx.at[c], rx.at[c], far).wait_recv()
        ys.append(send(full_ref.at[far_g, at], far_g, at, sy.at[c], ry.at[c], side))
        cs.append(send(full_ref.at[far_g, at], far_g, at, sc.at[0, c], rc.at[0, c], core))
    for c in range(lay.chunks):
        at = rows(1 - half, c)
        arrival(far_g, at, sy.at[c], ry.at[c], side).wait_recv()
        cs.append(send(full_ref.at[far_g, at], far_g, at, sc.at[1, c], rc.at[1, c], core))
    for copy in xs + ys:
        copy.wait_send()
    for copy in cs:
        copy.wait()
    own.wait()
    mine.wait()


def gather(lay, own):
    n = lay.chunks
    dma = pltpu.SemaphoreType.DMA
    return pl.pallas_call(
        functools.partial(gather_kernel, lay),
        out_shape=jax.ShapeDtypeStruct((lay.group, lay.padded, LANES), F32),
        in_specs=[pl.BlockSpec(memory_space=pl.ANY)],
        out_specs=pl.BlockSpec(memory_space=pl.ANY),
        scratch_shapes=[
            dma((n,)), dma((n,)), dma((n,)), dma((n,)), dma((2, n)), dma((2, n)), dma, dma, dma,
        ],
        compiler_params=pltpu.CompilerParams(collective_id=0, has_side_effects=True),
        name="gather_params",
    )(own)


def reduce_kernel(lay, grad_ref, out_ref, near, total, shifted, far_in, half_in, s_sem, r_sem):
    d, g = lax.axis_index("dp"), lax.axis_index("group")
    x, core = g // 2, g % 2
    bits = []
    step = 1
    while step < lay.dp:
        bits.append((d // step) % 2)
        step *= 2
    core_dev = {"dp": d, "group": 2 * x + 1 - core}
    far_dev = {"dp": d, "group": 2 * (1 - x) + core}
    dp_dev = [{"dp": d + (1 - 2 * b) * 2**k, "group": g} for k, b in enumerate(bits)]
    barrier = pltpu.get_barrier_semaphore()
    partners = [core_dev, far_dev] + dp_dev
    for other in partners:
        pl.semaphore_signal(barrier, inc=1, device_id=other, device_id_type=MESH)
    pl.semaphore_wait(barrier, len(partners))

    levels = len(bits)
    size = lay.chunk
    keep = [0]
    for k in range(levels):
        keep.append(keep[k] + bits[k] * (size >> (k + 1)))
    recv_at = []
    base = 0
    for k in range(levels):
        recv_at.append(base)
        base += size >> (k + 1)

    started = {}

    def send(phase, c, src, dst, other):
        copy = pltpu.make_async_remote_copy(
            src_ref=src,
            dst_ref=dst,
            send_sem=s_sem.at[phase, c],
            recv_sem=r_sem.at[phase, c],
            device_id=other,
            device_id_type=MESH,
        )
        copy.start()
        started[phase, c] = copy

    def at(offset, count):
        return pl.ds(pl.multiple_of(offset, 8), count)

    def stage(phase, c):
        begin = c * size
        whole = pl.ds(begin, size)
        if phase > 0:
            started[phase - 1, c].wait_recv()
        if phase == 0:
            send(0, c, grad_ref.at[:, 1 - core, whole], near.at[:, whole], core_dev)
        elif phase == 1:
            shifted[whole] = grad_ref[1 - x, core, whole] + near[1 - x, whole]
            send(1, c, shifted.at[whole], far_in.at[whole], far_dev)
        elif phase < 2 + levels:
            k = phase - 2
            part = size >> k
            if k == 0:
                total[whole] = grad_ref[x, core, whole] + near[x, whole] + far_in[whole]
            else:
                here = at(begin + keep[k], part)
                total[here] = total[here] + half_in[c, recv_at[k - 1] : recv_at[k - 1] + part]
            half = part // 2
            other = keep[k] + (1 - bits[k]) * half
            send(
                phase,
                c,
                total.at[at(begin + other, half)],
                half_in.at[c, recv_at[k] : recv_at[k] + half],
                dp_dev[k],
            )
        else:
            k = levels - 1 - (phase - 2 - levels)
            if k == levels - 1:
                part = size >> levels
                here = at(begin + keep[levels], part)
                out_ref[here] = total[here] + half_in[c, recv_at[k] : recv_at[k] + part]
            if k >= 0:
                here = at(begin + keep[k + 1], size >> (k + 1))
                send(phase, c, out_ref.at[here], out_ref.at[here], dp_dev[k])

    last = 2 + 2 * levels
    for turn in range(lay.chunks + last):
        for phase in range(last, -1, -1):
            c = turn - phase
            if 0 <= c < lay.chunks:
                stage(phase, c)
    for copy in started.values():
        copy.wait_send()


def reduce(lay, grads):
    levels = lay.dp.bit_length() - 1
    phases = 2 + 2 * levels
    dma = pltpu.SemaphoreType.DMA
    parts = sum(lay.chunk >> (k + 1) for k in range(levels))
    vmem = pl.BlockSpec(memory_space=pltpu.VMEM)
    return pl.pallas_call(
        functools.partial(reduce_kernel, lay),
        out_shape=jax.ShapeDtypeStruct((lay.padded, LANES), F32),
        in_specs=[vmem],
        out_specs=vmem,
        scratch_shapes=[
            pltpu.VMEM((2, lay.padded, LANES), F32),
            pltpu.VMEM((lay.padded, LANES), F32),
            pltpu.VMEM((lay.padded, LANES), F32),
            pltpu.VMEM((lay.padded, LANES), F32),
            pltpu.VMEM((lay.chunks, parts, LANES), F32),
            dma((phases, lay.chunks)),
            dma((phases, lay.chunks)),
        ],
        compiler_params=pltpu.CompilerParams(
            collective_id=1, has_side_effects=True, vmem_limit_bytes=40 * 2**20
        ),
        name="reduce_grads",
    )(grads.reshape(2, 2, lay.padded, LANES))


def dot(a, b):
    return jnp.dot(a, b, preferred_element_type=F32)


def dot_nt(a, b):
    return lax.dot_general(a, b, (((1,), (1,)), ((), ())), preferred_element_type=F32)


def dot_tn(a, b):
    return lax.dot_general(a, b, (((0,), (0,)), ((), ())), preferred_element_type=F32)


def column_sum(v):
    return jnp.sum(v, axis=0, keepdims=True)


def norm(values):
    middle = jnp.mean(values, axis=-1, keepdims=True)
    off = values - middle
    spread = jnp.mean(off * off, axis=-1, keepdims=True)
    scaled = lax.rsqrt(spread + 1e-06)
    return off * scaled, scaled


def norm_back(upstream, unit, scaled, gain):
    inner = upstream * gain
    return scaled * (
        inner
        - jnp.mean(inner, axis=-1, keepdims=True)
        - unit * jnp.mean(inner * unit, axis=-1, keepdims=True)
    )


def block_kernel(
    lay, counts_ref, full_ref, image_ref, cot_ref, out_ref, gin_ref, grad_ref,
    w_in, w_out, w_up, w_down, stage, x_s, g_s, unit_a, low_a, q_s, k_s, v_s, probs_s,
    mixed_s, resid_s, gm_s, gp_s, gacc_s,
):
    slots, tokens, _ = image_ref.shape
    pad = x_s.shape[0] // slots

    def weight(name, dst):
        start = STARTS[name]
        rows, columns = dst.shape
        stride = columns // LANES
        for j in range(stride):
            found = lay.pieces(start + j, stride, rows)
            lanes = slice(j * LANES, (j + 1) * LANES)
            if len(found) == 1:
                at = found[0][0]
                dst[:, lanes] = full_ref[pl.ds(at, rows, stride=stride), :].astype(LOW)
            else:
                for at, i, n in found:
                    stage[i : i + n, :] = full_ref[pl.ds(at, n, stride=stride), :]
                dst[:, lanes] = stage[0:rows, :].astype(LOW)

    def vector(name, skip=0, columns=D):
        start = STARTS[name] + skip // LANES
        found = []
        for j in range(columns // LANES):
            at = lay.pieces(start + j, 1, 1)[0][0]
            found.append(full_ref[at : at + 1, :])
        return jnp.concatenate(found, axis=1)

    def put_vector(name, value, skip=0):
        start = STARTS[name] + skip // LANES
        for j in range(value.shape[1] // LANES):
            at = lay.pieces(start + j, 1, 1)[0][0]
            grad_ref[at : at + 1, :] = value[:, j * LANES : (j + 1) * LANES]

    def put_weight(name, stride, value, first_row=0, first_column=0):
        rows, columns = value.shape
        start = STARTS[name] + first_row * stride + first_column // LANES
        for j in range(columns // LANES):
            found = lay.pieces(start + j, stride, rows)
            part = value[:, j * LANES : (j + 1) * LANES]
            if len(found) == 1:
                grad_ref[pl.ds(found[0][0], rows, stride=stride), :] = part
            else:
                stage[0:rows, :] = part
                for at, i, n in found:
                    grad_ref[pl.ds(at, n, stride=stride), :] = stage[i : i + n, :]

    weight("input", w_in)
    weight("output", w_out)
    weight("up", w_up)
    weight("down", w_down)
    for s in range(lay.group):
        tail = s * lay.padded + lay.real
        grad_ref[tail : (s + 1) * lay.padded, :] = jnp.zeros((lay.padded - lay.real, LANES), F32)

    count = counts_ref[0]
    x_s[...] = jnp.zeros_like(x_s)
    g_s[...] = jnp.zeros_like(g_s)
    lives = []
    for b in range(slots):
        live = jnp.where(b < count, 1.0, 0.0).astype(F32)
        lives.append(live)
        x_s[b * pad : b * pad + tokens, :] = image_ref[b].astype(F32)
        g_s[b * pad : b * pad + tokens, :] = cot_ref[b].astype(F32) * live

    unit, scale_a = norm(x_s[...])
    unit_a[...] = unit
    low_a[...] = (unit * vector("gain_a") + vector("shift_a")).astype(LOW)
    q_s[...] = (dot(low_a[...], w_in[:, 0:D]) + vector("query_bias")).astype(LOW)
    k_s[...] = dot(low_a[...], w_in[:, D : 2 * D]).astype(LOW)
    v_s[...] = (dot(low_a[...], w_in[:, 2 * D :]) + vector("value_bias")).astype(LOW)

    factor = HEAD_DIM ** (-0.5)
    first = lax.broadcasted_iota(jnp.int32, (pad, LANES), 1) < HEAD_DIM
    valid = lax.broadcasted_iota(jnp.int32, (pad, pad), 1) < tokens
    zero = jnp.zeros((pad, LANES), LOW)

    def only(value, h):
        return jnp.where(first, value, zero) if h == 0 else jnp.where(first, zero, value)

    pairs = HEADS // 2
    for b in range(slots):
        rows = slice(b * pad, (b + 1) * pad)
        for p in range(pairs):
            lanes = slice(p * LANES, (p + 1) * LANES)
            q, k, v = q_s[rows, lanes], k_s[rows, lanes], v_s[rows, lanes]
            parts = []
            for h in range(2):
                scores = dot_nt(only(q, h), k) * factor
                scores = jnp.where(valid, scores, -jnp.inf)
                top = jnp.max(scores, axis=-1, keepdims=True)
                e = jnp.exp(scores - top)
                probs = e * (1.0 / jnp.sum(e, axis=-1, keepdims=True))
                probs_s[(b * pairs + p) * 2 + h] = probs
                parts.append(dot(probs.astype(LOW), v))
            mixed_s[rows, lanes] = jnp.where(first, parts[0], parts[1]).astype(LOW)

    residual = x_s[...] + dot(mixed_s[...], w_out[...]) + vector("output_bias")
    resid_s[...] = residual
    unit_b, scale_b = norm(residual)
    hidden = (unit_b * vector("gain_b") + vector("shift_b")).astype(LOW)
    grad_low = g_s[...].astype(LOW)
    final = resid_s[...] + vector("down_bias")
    for j in range(FF // D):
        at = slice(j * D, (j + 1) * D)
        pre = dot(hidden, w_up[:, at]) + vector("up_bias", j * D)
        cdf = 0.5 * (1.0 + lax.erf(pre * (1.0 / math.sqrt(2.0))))
        act = (pre * cdf).astype(LOW)
        density = jnp.exp(-0.5 * pre * pre) * (1.0 / math.sqrt(2.0 * math.pi))
        final = final + dot(act, w_down[at, :])
        grad_pre = dot_nt(grad_low, w_down[at, :]) * (cdf + pre * density)
        put_vector("up_bias", column_sum(grad_pre), j * D)
        grad_pre_low = grad_pre.astype(LOW)
        put_weight("down", D // LANES, dot_tn(act, grad_low), first_row=j * D)
        put_weight("up", FF // LANES, dot_tn(hidden, grad_pre_low), first_column=j * D)
        back = dot_nt(grad_pre_low, w_up[:, at])
        if j == 0:
            gacc_s[...] = back
        else:
            gacc_s[...] += back
    for b in range(slots):
        out_ref[b] = (final[b * pad : b * pad + tokens, :] * lives[b]).astype(LOW)
    put_vector("down_bias", column_sum(g_s[...]))

    grad_hidden = gacc_s[...]
    put_vector("gain_b", column_sum(grad_hidden * unit_b))
    put_vector("shift_b", column_sum(grad_hidden))
    grad_resid = g_s[...] + norm_back(grad_hidden, unit_b, scale_b, vector("gain_b"))
    resid_s[...] = grad_resid
    put_vector("output_bias", column_sum(grad_resid))
    resid_low = grad_resid.astype(LOW)
    put_weight("output", D // LANES, dot_tn(mixed_s[...], resid_low))
    gm_s[...] = dot_nt(resid_low, w_out[...]).astype(LOW)

    query_sum = [0.0] * pairs
    value_sum = [0.0] * pairs
    for b in range(slots):
        rows = slice(b * pad, (b + 1) * pad)
        for p in range(pairs):
            lanes = slice(p * LANES, (p + 1) * LANES)
            q, k, v, gm = q_s[rows, lanes], k_s[rows, lanes], v_s[rows, lanes], gm_s[rows, lanes]
            gq, gk, gv = [], [], []
            for h in range(2):
                probs = probs_s[(b * pairs + p) * 2 + h]
                grad_probs = dot_nt(only(gm, h), v)
                gv.append(dot_tn(probs.astype(LOW), gm))
                centre = jnp.sum(grad_probs * probs, axis=-1, keepdims=True)
                grad_scores = (probs * (grad_probs - centre) * factor).astype(LOW)
                gq.append(dot(grad_scores, k))
                gk.append(dot_tn(grad_scores, q))
            both = [jnp.where(first, pair[0], pair[1]) for pair in (gq, gk, gv)]
            query_sum[p] = query_sum[p] + column_sum(both[0])
            value_sum[p] = value_sum[p] + column_sum(both[2])
            for c in range(3):
                gp_s[rows, c * D + p * LANES : c * D + (p + 1) * LANES] = both[c].astype(LOW)
    put_vector("query_bias", jnp.concatenate(query_sum, axis=1))
    put_vector("value_bias", jnp.concatenate(value_sum, axis=1))
    for c in range(3):
        at = slice(c * D, (c + 1) * D)
        put_weight(
            "input", 3 * D // LANES, dot_tn(low_a[...], gp_s[:, at]), first_column=c * D
        )
    grad_normed = dot_nt(gp_s[...], w_in[...])
    put_vector("gain_a", column_sum(grad_normed * unit_a[...]))
    put_vector("shift_a", column_sum(grad_normed))
    grad_in = resid_s[...] + norm_back(grad_normed, unit_a[...], scale_a, vector("gain_a"))
    for b in range(slots):
        gin_ref[b] = grad_in[b * pad : b * pad + tokens, :].astype(LOW)


def block_pass(lay, full, images, upstream, counts):
    slots, tokens, _ = images.shape
    pad = -(-tokens // 16) * 16
    rows = slots * pad
    vmem = pl.BlockSpec(memory_space=pltpu.VMEM)
    flat = (lay.group * lay.padded, LANES)
    low = lambda *shape: pltpu.VMEM(shape, LOW)
    wide = lambda *shape: pltpu.VMEM(shape, F32)
    return pl.pallas_call(
        functools.partial(block_kernel, lay),
        out_shape=(
            jax.ShapeDtypeStruct(images.shape, LOW),
            jax.ShapeDtypeStruct(images.shape, LOW),
            jax.ShapeDtypeStruct(flat, F32),
        ),
        in_specs=[pl.BlockSpec(memory_space=pltpu.SMEM), vmem, vmem, vmem],
        out_specs=(vmem, vmem, vmem),
        scratch_shapes=[
            low(D, 3 * D), low(D, D), low(D, FF), low(FF, D), wide(FF, LANES),
            wide(rows, D), wide(rows, D), wide(rows, D), low(rows, D),
            low(rows, D), low(rows, D), low(rows, D),
            wide(slots * HEADS, pad, pad),
            low(rows, D), wide(rows, D), low(rows, D), low(rows, 3 * D), wide(rows, D),
        ],
        compiler_params=pltpu.CompilerParams(vmem_limit_bytes=56 * 2**20),
        name="block_pass",
    )(counts, full.reshape(flat), images, upstream)


def adamw_update(weights, first_moment, second_moment, gradient):
    first_new = 0.9 * first_moment + 0.1 * gradient
    second_new = 0.99 * second_moment + 0.01 * gradient * gradient
    first_hat = first_new / (1.0 - 0.9**STEP)
    second_hat = second_new / (1.0 - 0.99**STEP)
    weights_new = weights - 0.02 * (first_hat / (jnp.sqrt(second_hat) + 1e-08) + 0.05 * weights)
    return (weights_new, first_new, second_new)


def on_device(params, moment1, moment2, image_in, cotangent, image_counts):
    group, dp = lax.axis_size("group"), lax.axis_size("dp")
    lay = Layout(params.shape[0], group, dp)
    own = jnp.pad(params, (0, (lay.padded - lay.real) * LANES)).reshape(lay.padded, LANES)
    full = gather(lay, own)
    outputs, grad_inputs, grads = block_pass(lay, full, image_in, cotangent, image_counts)
    summed = reduce(lay, grads)
    images = image_in.shape[0] * group * dp
    grad_shard = summed.reshape(-1)[: params.shape[0]] * (1.0 / images)
    new_params, new_first, new_second = adamw_update(params, moment1, moment2, grad_shard)
    return (outputs, grad_inputs, grad_shard, new_params, new_first, new_second)


def solution(mesh):
    placed = (
        P("group"),
        P("group"),
        P("group"),
        P(("dp", "group"), None, None),
        P(("dp", "group"), None, None),
        P(("dp", "group")),
    )
    return jax.shard_map(
        on_device,
        mesh=mesh,
        in_specs=placed,
        out_specs=(
            P(("dp", "group"), None, None),
            P(("dp", "group"), None, None),
            P("group"),
            P("group"),
            P("group"),
            P("group"),
        ),
        check_vma=False,
    )
```

profile of v0, /device:TPU:0, one launch (start us, length us, event | category | flops | bytes accessed | tf_op | source)
XLA Modules:
  0.0 181.1 jit_solution(5053971579935001850)
XLA Ops:
  1.3 1.7 copy.12.image_ref
  3.0 1.7 copy.13.cot_ref
  4.7 2.9 %pad_bitcast_fusion.own_ref = f32[3520,128]{1,0:T(8,128)} fusion(f32[443520]{0:T(1024)} %param.6), kind=kLoop, calls=%fused_computation | loop fusion | bytes 3576320 | tf_op jit(solution)/shard_map/reshape | solution.py:527
  7.6 59.5 %gather_params.1 = f32[4,3520,128]{2,1,0:T(8,128)} custom-call(f32[3520,128]{1,0:T(8,128)} %pad_bitcast_fusion.own_ref), custom_call_target="tpu_custom_call" | custom-call | tf_op jit(solution)/shard_map/gather_params/pallas_call | solution.py:148
  67.1 20.8 %block_pass.1 = (bf16[2,197,384]{2,1,0:T(8,128)(2,1)}, bf16[2,197,384]{2,1,0:T(8,128)(2,1)}, f32[14080,128]{1,0:T(8,128)}) custom-call(s32[1]{0:T(128)S(6)} %copy.16.counts_ref, f32[14080,128]{1,0:T(8,128)} %bitcast.16, bf16[2,197,384]{2,1,0:T(8,128)(2,1)} %copy.12.image_ref, bf16[2,197,384]{2,1,0:T(8,128)(2,1)} %copy.13.cot_ref), custom_call_target="tpu_custom_call" | custom-call | tf_op jit(solution)/shard_map/block_pass/pallas_call | solution.py:494
  87.9 1.9 %copy.14 = bf16[2,197,384]{2,0,1:T(2,128)(2,1)} copy(bf16[2,197,384]{2,1,0:T(8,128)(2,1)} %get-tuple-element.12) | data formatting | bytes 605184
  89.8 1.9 %copy.15 = bf16[2,197,384]{2,0,1:T(2,128)(2,1)} copy(bf16[2,197,384]{2,1,0:T(8,128)(2,1)} %get-tuple-element.13) | data formatting | bytes 605184
  91.8 0.0 copy-start
  91.8 3.0 %copy-done = f32[14080,128]{1,0:T(8,128)S(1)} copy-done((f32[14080,128]{1,0:T(8,128)S(1)}, f32[14080,128]{1,0:T(8,128)}, u32[]{:S(2)}) %copy-start) | copy-done | bytes 7208984
  94.8 0.0 copy-start.1
  94.8 0.0 copy-start.2
  94.8 0.0 copy-start.3
  94.8 82.3 %reduce_grads.1 = f32[3520,128]{1,0:T(8,128)S(1)} custom-call(f32[2,2,3520,128]{3,2,1,0:T(8,128)S(1)} %bitcast.15), custom_call_target="tpu_custom_call" | custom-call | tf_op jit(solution)/shard_map/reduce_grads/pallas_call | solution.py:259
  177.1 0.0 copy-done.1
  177.1 0.0 copy-done.2
  177.1 0.0 copy-done.3
  177.1 4.0 %multiply_subtract_fusion = (f32[443520]{0:T(1024)}, f32[443520]{0:T(1024)}, f32[443520]{0:T(1024)}, f32[443520]{0:T(1024)}) fusion(f32[443520]{0:T(1024)S(1)} %copy-done.1, f32[3520,128]{1,0:T(8,128)S(1)} %reduce_grads.1, f32[443520]{0:T(1024)S(1)} %copy-done.2, f32[443520]{0:T(1024)S(1)} %copy-done.3), kind=kLoop, calls=%fused_computation.4 | loop fusion | flops 7096320 | bytes 14192640 | tf_op jit(solution)/shard_map/sub | solution.py:520
Async XLA Ops:
  91.8 3.0 %copy-start = (f32[14080,128]{1,0:T(8,128)S(1)}, f32[14080,128]{1,0:T(8,128)}, u32[]{:S(2)}) copy-start(f32[14080,128]{1,0:T(8,128)} %get-tuple-element.11) | copy-start | bytes 21626884
  94.8 82.3 %copy-start.1 = (f32[443520]{0:T(1024)S(1)}, f32[443520]{0:T(1024)}, u32[]{:S(2)}) copy-start(f32[443520]{0:T(1024)} %param.6) | copy-start | bytes 5322244
  94.8 82.3 %copy-start.2 = (f32[443520]{0:T(1024)S(1)}, f32[443520]{0:T(1024)}, u32[]{:S(2)}) copy-start(f32[443520]{0:T(1024)} %param.7) | copy-start | bytes 5322244
  94.8 82.3 %copy-start.3 = (f32[443520]{0:T(1024)S(1)}, f32[443520]{0:T(1024)}, u32[]{:S(2)}) copy-start(f32[443520]{0:T(1024)} %param.8) | copy-start | bytes 5322244
where the time goes:
time: 181 us
  Pallas kernels  163 us (90%)
  local copies, waits for them, and re-layouts  13.2 us (7%)
  other arithmetic  4.02 us (2%)
    pallas_call x1, Pallas kernels, reduce(): pl.pallas_call(functools.partial(reduce_kernel, lay), out_shape=jax.Shape...  82.3 us
    pallas_call x1, Pallas kernels, gather(): pl.pallas_call(functools.partial(gather_kernel, lay), out_shape=jax.Shape...  59.5 us
    pallas_call x1, Pallas kernels, block_pass(): pl.pallas_call(functools.partial(block_kernel, lay), out_shape=(jax.Shape...  20.8 us
    unnamed x12, local copies, waits for them, and re-layouts  10.3 us
    sub x1, other arithmetic, adamw_update(): weights - 0.02 * (first_hat / (jnp.sqrt(second_hat) + 1e-08) + 0.05 * wei...  4.02 us

commit v1 on v0

--- a/solution.py
+++ b/solution.py
@@ -14,6 +14,12 @@
 FF = 1536
 STEP = 5
 LANES = 128
+MOST_CHUNKS = 14
+MOST_PARTS = 8
+IN_FLIGHT = 2
+FAR_AHEAD = 2
+SIDE_AHEAD = 2
+WIDE_AHEAD = 2
 MESH = pl.DeviceIdType.MESH
 LOW = jnp.bfloat16
 F32 = jnp.float32
@@ -52,10 +58,17 @@
         self.group = group
         self.dp = dp
         unit = 8 * dp
-        units = -(-self.real // unit)
-        self.chunks = max(n for n in range(1, 12) if units % n == 0)
-        self.padded = units * unit
+        least = -(-self.real // unit)
+        self.chunks, units = max(
+            (n, -units)
+            for units in range(least, least + least // 16 + 1)
+            for n in range(1, MOST_CHUNKS + 1)
+            if units % n == 0
+        )
+        self.padded = -units * unit
         self.chunk = self.padded // self.chunks
+        half = self.padded // 16
+        self.parts = max(n for n in range(1, MOST_PARTS + 1) if half % n == 0)
 
     def pieces(self, start, stride, count):
         i, found = 0, []
@@ -80,7 +93,7 @@
         pl.semaphore_signal(barrier, inc=1, device_id=other, device_id_type=MESH)
     pl.semaphore_wait(barrier, 3)
 
-    piece = lay.chunk // 2
+    piece = lay.padded // 2 // lay.parts
     half_rows = lay.padded // 2
 
     def rows(which, c):
@@ -108,11 +121,25 @@
             device_id_type=MESH,
         )
 
-    sends = []
-    xs = []
-    for c in range(lay.chunks):
+    xs, ys, cs = [], [], []
+
+    def send_far(c):
         at = rows(half, c)
         xs.append(send(own_ref.at[at], g, at, sx.at[c], rx.at[c], far))
+
+    def pass_far(c):
+        at = rows(half, c)
+        arrival(far_g, at, sx.at[c], rx.at[c], far).wait_recv()
+        ys.append(send(full_ref.at[far_g, at], far_g, at, sy.at[c], ry.at[c], side))
+        cs.append(send(full_ref.at[far_g, at], far_g, at, sc.at[0, c], rc.at[0, c], core))
+
+    def pass_side(c):
+        at = rows(1 - half, c)
+        arrival(far_g, at, sy.at[c], ry.at[c], side).wait_recv()
+        cs.append(send(full_ref.at[far_g, at], far_g, at, sc.at[1, c], rc.at[1, c], core))
+
+    for c in range(min(IN_FLIGHT, lay.parts)):
+        send_far(c)
     mine = pltpu.make_async_copy(own_ref, full_ref.at[g], local_sem)
     mine.start()
     own = pltpu.make_async_remote_copy(
@@ -124,16 +151,14 @@
         device_id_type=MESH,
     )
     own.start()
-    ys, cs = [], []
-    for c in range(lay.chunks):
-        at = rows(half, c)
-        arrival(far_g, at, sx.at[c], rx.at[c], far).wait_recv()
-        ys.append(send(full_ref.at[far_g, at], far_g, at, sy.at[c], ry.at[c], side))
-        cs.append(send(full_ref.at[far_g, at], far_g, at, sc.at[0, c], rc.at[0, c], core))
-    for c in range(lay.chunks):
-        at = rows(1 - half, c)
-        arrival(far_g, at, sy.at[c], ry.at[c], side).wait_recv()
-        cs.append(send(full_ref.at[far_g, at], far_g, at, sc.at[1, c], rc.at[1, c], core))
+    for c in range(lay.parts):
+        pass_far(c)
+        if c + IN_FLIGHT < lay.parts:
+            send_far(c + IN_FLIGHT)
+        if c >= IN_FLIGHT:
+            pass_side(c - IN_FLIGHT)
+    for c in range(max(lay.parts - IN_FLIGHT, 0), lay.parts):
+        pass_side(c)
     for copy in xs + ys:
         copy.wait_send()
     for copy in cs:
@@ -143,12 +168,12 @@
 
 
 def gather(lay, own):
-    n = lay.chunks
+    n = lay.parts
     dma = pltpu.SemaphoreType.DMA
     return pl.pallas_call(
         functools.partial(gather_kernel, lay),
         out_shape=jax.ShapeDtypeStruct((lay.group, lay.padded, LANES), F32),
-        in_specs=[pl.BlockSpec(memory_space=pl.ANY)],
+        in_specs=[pl.BlockSpec(memory_space=pltpu.VMEM)],
         out_specs=pl.BlockSpec(memory_space=pl.ANY),
         scratch_shapes=[
             dma((n,)), dma((n,)), dma((n,)), dma((n,)), dma((2, n)), dma((2, n)), dma, dma, dma,
@@ -158,103 +183,131 @@
     )(own)
 
 
-def reduce_kernel(lay, grad_ref, out_ref, near, total, shifted, far_in, half_in, s_sem, r_sem):
+def radices_of(dp):
+    found, rest = [], dp
+    if rest % 2 == 0:
+        found.append(2)
+        rest //= 2
+    while rest > 1:
+        r = next(n for n in (4, 2, rest) if rest % n == 0)
+        found.append(r)
+        rest //= r
+    return found
+
+
+def reduce_kernel(lay, grad_ref, out_ref, near, total, shifted, far_in, part_in, s_sem, r_sem):
     d, g = lax.axis_index("dp"), lax.axis_index("group")
     x, core = g // 2, g % 2
-    bits = []
-    step = 1
-    while step < lay.dp:
-        bits.append((d // step) % 2)
-        step *= 2
     core_dev = {"dp": d, "group": 2 * x + 1 - core}
     far_dev = {"dp": d, "group": 2 * (1 - x) + core}
-    dp_dev = [{"dp": d + (1 - 2 * b) * 2**k, "group": g} for k, b in enumerate(bits)]
+    levels, step = [], 1
+    for radix in radices_of(lay.dp):
+        digit = (d // step) % radix
+        others = []
+        for o in range(1, radix):
+            digit_o = (digit + o) % radix
+            others.append((digit_o, {"dp": d + (digit_o - digit) * step, "group": g}))
+        levels.append((radix, digit, others))
+        step *= radix
     barrier = pltpu.get_barrier_semaphore()
-    partners = [core_dev, far_dev] + dp_dev
+    partners = [core_dev, far_dev] + [dev for _, _, others in levels for _, dev in others]
     for other in partners:
         pl.semaphore_signal(barrier, inc=1, device_id=other, device_id_type=MESH)
     pl.semaphore_wait(barrier, len(partners))
 
-    levels = len(bits)
-    size = lay.chunk
-    keep = [0]
-    for k in range(levels):
-        keep.append(keep[k] + bits[k] * (size >> (k + 1)))
-    recv_at = []
-    base = 0
-    for k in range(levels):
-        recv_at.append(base)
-        base += size >> (k + 1)
-
+    depth = len(levels)
+    held, keep, slot, base = [lay.chunk], [0], [], 0
+    for radix, digit, others in levels:
+        part = held[-1] // radix
+        keep.append(keep[-1] + digit * part)
+        held.append(part)
+        slot.append(base)
+        base += part * (radix - 1)
     started = {}
-
-    def send(phase, c, src, dst, other):
+    sems = {}
+
+    def send(phase, o, c, src, dst, other):
+        at = sems.setdefault((phase, o), len(sems))
         copy = pltpu.make_async_remote_copy(
             src_ref=src,
             dst_ref=dst,
-            send_sem=s_sem.at[phase, c],
-            recv_sem=r_sem.at[phase, c],
+            send_sem=s_sem.at[at, c],
+            recv_sem=r_sem.at[at, c],
             device_id=other,
             device_id_type=MESH,
         )
         copy.start()
-        started[phase, c] = copy
+        started.setdefault((phase, c), []).append(copy)
 
     def at(offset, count):
         return pl.ds(pl.multiple_of(offset, 8), count)
 
+    def arrived(k, c):
+        radix, part = levels[k][0], held[k + 1]
+        found = [part_in[c, slot[k] + o * part : slot[k] + (o + 1) * part] for o in range(radix - 1)]
+        return functools.reduce(lambda a, b: a + b, found)
+
     def stage(phase, c):
-        begin = c * size
-        whole = pl.ds(begin, size)
-        if phase > 0:
-            started[phase - 1, c].wait_recv()
+        begin = c * lay.chunk
+        whole = pl.ds(begin, lay.chunk)
+        for copy in started.get((phase - 1, c), []):
+            copy.wait_recv()
         if phase == 0:
-            send(0, c, grad_ref.at[:, 1 - core, whole], near.at[:, whole], core_dev)
+            send(0, 0, c, grad_ref.at[:, 1 - core, whole], near.at[:, whole], core_dev)
         elif phase == 1:
             shifted[whole] = grad_ref[1 - x, core, whole] + near[1 - x, whole]
-            send(1, c, shifted.at[whole], far_in.at[whole], far_dev)
-        elif phase < 2 + levels:
+            send(1, 0, c, shifted.at[whole], far_in.at[whole], far_dev)
+        elif phase < 2 + depth:
             k = phase - 2
-            part = size >> k
             if k == 0:
                 total[whole] = grad_ref[x, core, whole] + near[x, whole] + far_in[whole]
             else:
-                here = at(begin + keep[k], part)
-                total[here] = total[here] + half_in[c, recv_at[k - 1] : recv_at[k - 1] + part]
-            half = part // 2
-            other = keep[k] + (1 - bits[k]) * half
-            send(
-                phase,
-                c,
-                total.at[at(begin + other, half)],
-                half_in.at[c, recv_at[k] : recv_at[k] + half],
-                dp_dev[k],
-            )
+                here = at(begin + keep[k], held[k])
+                total[here] = total[here] + arrived(k - 1, c)
+            part = held[k + 1]
+            for o, (digit, dev) in enumerate(levels[k][2]):
+                send(
+                    phase,
+                    o,
+                    c,
+                    total.at[at(begin + keep[k] + digit * part, part)],
+                    part_in.at[c, slot[k] + o * part : slot[k] + (o + 1) * part],
+                    dev,
+                )
         else:
-            k = levels - 1 - (phase - 2 - levels)
-            if k == levels - 1:
-                part = size >> levels
-                here = at(begin + keep[levels], part)
-                out_ref[here] = total[here] + half_in[c, recv_at[k] : recv_at[k] + part]
+            k = depth - 1 - (phase - 2 - depth)
+            if k == depth - 1:
+                here = at(begin + keep[depth], held[depth])
+                out_ref[here] = total[here] + arrived(k, c)
             if k >= 0:
-                here = at(begin + keep[k + 1], size >> (k + 1))
-                send(phase, c, out_ref.at[here], out_ref.at[here], dp_dev[k])
-
-    last = 2 + 2 * levels
-    for turn in range(lay.chunks + last):
-        for phase in range(last, -1, -1):
-            c = turn - phase
+                here = at(begin + keep[k + 1], held[k + 1])
+                for o, (_, dev) in enumerate(levels[k][2]):
+                    send(phase, o, c, out_ref.at[here], out_ref.at[here], dev)
+
+    last = 2 + 2 * depth
+    late = [0, 1, 1 + FAR_AHEAD, 1 + FAR_AHEAD + SIDE_AHEAD]
+    while len(late) < last:
+        late.append(late[-1] + WIDE_AHEAD)
+    late.append(late[-1] + SIDE_AHEAD)
+    order = [1, 0] + list(range(last, 1, -1))
+    for turn in range(lay.chunks + late[last]):
+        for phase in order:
+            c = turn - late[phase]
             if 0 <= c < lay.chunks:
                 stage(phase, c)
-    for copy in started.values():
-        copy.wait_send()
+    for copies in started.values():
+        for copy in copies:
+            copy.wait_send()
 
 
 def reduce(lay, grads):
-    levels = lay.dp.bit_length() - 1
-    phases = 2 + 2 * levels
+    radices = radices_of(lay.dp)
+    copies = 2 + 2 * sum(r - 1 for r in radices)
+    parts, held = 0, lay.chunk
+    for r in radices:
+        held //= r
+        parts += held * (r - 1)
     dma = pltpu.SemaphoreType.DMA
-    parts = sum(lay.chunk >> (k + 1) for k in range(levels))
     vmem = pl.BlockSpec(memory_space=pltpu.VMEM)
     return pl.pallas_call(
         functools.partial(reduce_kernel, lay),
@@ -267,11 +320,11 @@
             pltpu.VMEM((lay.padded, LANES), F32),
             pltpu.VMEM((lay.padded, LANES), F32),
             pltpu.VMEM((lay.chunks, parts, LANES), F32),
-            dma((phases, lay.chunks)),
-            dma((phases, lay.chunks)),
+            dma((copies, lay.chunks)),
+            dma((copies, lay.chunks)),
         ],
         compiler_params=pltpu.CompilerParams(
-            collective_id=1, has_side_effects=True, vmem_limit_bytes=40 * 2**20
+            collective_id=1, has_side_effects=True, vmem_limit_bytes=28 * 2**20
         ),
         name="reduce_grads",
     )(grads.reshape(2, 2, lay.padded, LANES))
@@ -315,7 +368,7 @@
     w_in, w_out, w_up, w_down, stage, x_s, g_s, unit_a, low_a, q_s, k_s, v_s, probs_s,
     mixed_s, resid_s, gm_s, gp_s, gacc_s,
 ):
-    slots, tokens, _ = image_ref.shape
+    tokens, slots, _ = image_ref.shape
     pad = x_s.shape[0] // slots
 
     def weight(name, dst):
@@ -375,8 +428,8 @@
     for b in range(slots):
         live = jnp.where(b < count, 1.0, 0.0).astype(F32)
         lives.append(live)
-        x_s[b * pad : b * pad + tokens, :] = image_ref[b].astype(F32)
-        g_s[b * pad : b * pad + tokens, :] = cot_ref[b].astype(F32) * live
+        x_s[b * pad : b * pad + tokens, :] = image_ref[:, b, :].astype(F32)
+        g_s[b * pad : b * pad + tokens, :] = cot_ref[:, b, :].astype(F32) * live
 
     unit, scale_a = norm(x_s[...])
     unit_a[...] = unit
@@ -434,7 +487,7 @@
         else:
             gacc_s[...] += back
     for b in range(slots):
-        out_ref[b] = (final[b * pad : b * pad + tokens, :] * lives[b]).astype(LOW)
+        out_ref[:, b, :] = (final[b * pad : b * pad + tokens, :] * lives[b]).astype(LOW)
     put_vector("down_bias", column_sum(g_s[...]))
 
     grad_hidden = gacc_s[...]
@@ -480,11 +533,11 @@
     put_vector("shift_a", column_sum(grad_normed))
     grad_in = resid_s[...] + norm_back(grad_normed, unit_a[...], scale_a, vector("gain_a"))
     for b in range(slots):
-        gin_ref[b] = grad_in[b * pad : b * pad + tokens, :].astype(LOW)
+        gin_ref[:, b, :] = grad_in[b * pad : b * pad + tokens, :].astype(LOW)
 
 
 def block_pass(lay, full, images, upstream, counts):
-    slots, tokens, _ = images.shape
+    tokens, slots, _ = images.shape
     pad = -(-tokens // 16) * 16
     rows = slots * pad
     vmem = pl.BlockSpec(memory_space=pltpu.VMEM)
@@ -507,7 +560,7 @@
             wide(slots * HEADS, pad, pad),
             low(rows, D), wide(rows, D), low(rows, D), low(rows, 3 * D), wide(rows, D),
         ],
-        compiler_params=pltpu.CompilerParams(vmem_limit_bytes=56 * 2**20),
+        compiler_params=pltpu.CompilerParams(vmem_limit_bytes=40 * 2**20),
         name="block_pass",
     )(counts, full.reshape(flat), images, upstream)
 
@@ -526,10 +579,12 @@
     lay = Layout(params.shape[0], group, dp)
     own = jnp.pad(params, (0, (lay.padded - lay.real) * LANES)).reshape(lay.padded, LANES)
     full = gather(lay, own)
-    outputs, grad_inputs, grads = block_pass(lay, full, image_in, cotangent, image_counts)
+    images, upstream = (jnp.swapaxes(v, 0, 1) for v in (image_in, cotangent))
+    outputs, grad_inputs, grads = block_pass(lay, full, images, upstream, image_counts)
+    outputs, grad_inputs = (jnp.swapaxes(v, 0, 1) for v in (outputs, grad_inputs))
     summed = reduce(lay, grads)
-    images = image_in.shape[0] * group * dp
-    grad_shard = summed.reshape(-1)[: params.shape[0]] * (1.0 / images)
+    count = image_in.shape[0] * group * dp
+    grad_shard = summed.reshape(-1)[: params.shape[0]] * (1.0 / count)
     new_params, new_first, new_second = adamw_update(params, moment1, moment2, grad_shard)
     return (outputs, grad_inputs, grad_shard, new_params, new_first, new_second)
 

time: 181 us -> 125 us (0.69)
  Pallas kernels: 163 us -> 116 us
  local copies, waits for them, and re-layouts: 13.2 us -> 2.93 us
    pallas_call x1, Pallas kernels: 59.5 us -> 32.8 us  [gather(): pl.pallas_call(functools.partial(gather_kernel, lay), out_shape=jax.Shape...]
    pallas_call x1, Pallas kernels: 82.3 us -> 64.2 us  [reduce(): pl.pallas_call(functools.partial(reduce_kernel, lay), out_shape=jax.Shape...]
    unnamed x12 -> x10, local copies, waits for them, and re-layouts: 10.3 us -> 0.02 us
where the time goes in v1:
time: 125 us; the launch traced here: 124 us
  Pallas kernels  116 us (93%)
  other arithmetic  4.09 us (3%)
  local copies, waits for them, and re-layouts  2.93 us (2%)
  between operations  1.34 us (1%)
    pallas_call x1, Pallas kernels, reduce(): pl.pallas_call(functools.partial(reduce_kernel, lay), out_shape=jax.Shape...  64.2 us
    pallas_call x1, Pallas kernels, gather(): pl.pallas_call(functools.partial(gather_kernel, lay), out_shape=jax.Shape...  32.8 us
    pallas_call x1, Pallas kernels, block_pass(): pl.pallas_call(functools.partial(block_kernel, lay), out_shape=(jax.Shape...  19.1 us
    sub x1, other arithmetic, adamw_update(): weights - 0.02 * (first_hat / (jnp.sqrt(second_hat) + 1e-08) + 0.05 * wei...  4.09 us
    reshape x1, local copies, waits for them, and re-layouts, on_device(): jnp.pad(params, (0, (lay.padded - lay.real) * LANES))  2.91 us

profile of v1, /device:TPU:0, one launch (start us, length us, event | category | flops | bytes accessed | tf_op | source)
XLA Modules:
  0.0 124.5 jit_solution(8116575052078182775)
XLA Ops:
  1.3 2.9 %pad_bitcast_fusion.own_ref = f32[3584,128]{1,0:T(8,128)} fusion(f32[443520]{0:T(1024)} %param.6), kind=kLoop, calls=%fused_computation | loop fusion | bytes 3609088 | tf_op jit(solution)/shard_map/reshape | solution.py:580
  4.2 0.0 copy-start
  4.2 0.0 copy-start.1
  4.2 32.8 %gather_params.1 = f32[4,3584,128]{2,1,0:T(8,128)} custom-call(f32[3584,128]{1,0:T(8,128)} %pad_bitcast_fusion.own_ref), custom_call_target="tpu_custom_call" | custom-call | tf_op jit(solution)/shard_map/gather_params/pallas_call | solution.py:173
  37.0 0.0 copy-done
  37.0 0.0 copy-done.1
  37.0 19.1 %block_pass.1 = (bf16[197,2,384]{2,1,0:T(2,128)(2,1)}, bf16[197,2,384]{2,1,0:T(2,128)(2,1)}, f32[14336,128]{1,0:T(8,128)S(1)}) custom-call(s32[1]{0:T(128)S(6)} %copy.12.counts_ref, f32[14336,128]{1,0:T(8,128)} %bitcast.22, bf16[197,2,384]{2,1,0:T(2,128)(2,1)S(1)} %bitcast.20, bf16[197,2,384]{2,1,0:T(2,128)(2,1)S(1)} %bitcast.21), custom_call_target="tpu_custom_call" | custom-call | tf_op jit(solution)/shard_map/block_pass/pallas_call | solution.py:547
  56.1 0.0 copy-start.2
  56.1 0.0 copy-start.3
  56.1 0.0 copy-start.4
  56.1 64.2 %reduce_grads.1 = f32[3584,128]{1,0:T(8,128)S(1)} custom-call(f32[2,2,3584,128]{3,2,1,0:T(8,128)S(1)} %bitcast.19), custom_call_target="tpu_custom_call" | custom-call | tf_op jit(solution)/shard_map/reduce_grads/pallas_call | solution.py:312
  120.4 0.0 copy-done.2
  120.4 0.0 copy-done.3
  120.4 0.0 copy-done.4
  120.4 4.1 %multiply_subtract_fusion = (f32[443520]{0:T(1024)}, f32[443520]{0:T(1024)}, f32[443520]{0:T(1024)}, f32[443520]{0:T(1024)}) fusion(f32[443520]{0:T(1024)S(1)} %copy-done.2, f32[3584,128]{1,0:T(8,128)S(1)} %reduce_grads.1, f32[443520]{0:T(1024)S(1)} %copy-done.3, f32[443520]{0:T(1024)S(1)} %copy-done.4), kind=kLoop, calls=%fused_computation.4 | loop fusion | flops 7096320 | bytes 14192640 | tf_op jit(solution)/shard_map/sub | solution.py:573
Async XLA Ops:
  4.2 32.8 %copy-start = (bf16[2,197,384]{2,0,1:T(2,128)(2,1)S(1)}, bf16[2,197,384]{2,0,1:T(2,128)(2,1)}, u32[]{:S(2)}) copy-start(bf16[2,197,384]{2,0,1:T(2,128)(2,1)} %param.9) | copy-start | bytes 907780
  4.2 32.8 %copy-start.1 = (bf16[2,197,384]{2,0,1:T(2,128)(2,1)S(1)}, bf16[2,197,384]{2,0,1:T(2,128)(2,1)}, u32[]{:S(2)}) copy-start(bf16[2,197,384]{2,0,1:T(2,128)(2,1)} %param.10) | copy-start | bytes 907780
  56.1 64.3 %copy-start.2 = (f32[443520]{0:T(1024)S(1)}, f32[443520]{0:T(1024)}, u32[]{:S(2)}) copy-start(f32[443520]{0:T(1024)} %param.6) | copy-start | bytes 5322244
  56.1 64.3 %copy-start.3 = (f32[443520]{0:T(1024)S(1)}, f32[443520]{0:T(1024)}, u32[]{:S(2)}) copy-start(f32[443520]{0:T(1024)} %param.7) | copy-start | bytes 5322244
  56.1 64.3 %copy-start.4 = (f32[443520]{0:T(1024)S(1)}, f32[443520]{0:T(1024)}, u32[]{:S(2)}) copy-start(f32[443520]{0:T(1024)} %param.8) | copy-start | bytes 5322244
